TPU v7x, 32 devices: a whole 2x2x4 slice. The times are simulated.
32 devices in a mesh: groups: 2 (over y), row: 4 (over z), col: 2 (over x), rep: 2 (over core).
Axes of the slice: x: 2, y: 2, z: 4, core: 2. Of those that a mesh axis runs over, the one named last changes fastest.
Arguments:
- tokens: bfloat16 [256, 8192], P(('groups', 'row', 'rep'), 'col'), parts along dimension 0, may hold values from -6 to 6
- gate_blocks: bfloat16 [64, 4, 24, 128, 128], P('col', 'row'), may hold values from -0.09375 to 0.09375
- gate_cols: int32 [64, 4, 24], P('col', 'row'), may hold values from 0 to 31, as said below
- gate_count: int32 [64, 4], P('col', 'row'), may hold values from 8 to 24, as said below
- up_blocks: bfloat16 [64, 4, 24, 128, 128], P('col', 'row'), may hold values from -0.09375 to 0.09375
- up_cols: int32 [64, 4, 24], P('col', 'row'), may hold values from 0 to 31, as said below
- up_count: int32 [64, 4], P('col', 'row'), may hold values from 8 to 24, as said below
- down_blocks: bfloat16 [128, 2, 24, 128, 128], P('row', 'col'), may hold values from -0.0625 to 0.0625
- down_cols: int32 [128, 2, 24], P('row', 'col'), may hold values from 0 to 31, as said below
- down_count: int32 [128, 2], P('row', 'col'), may hold values from 8 to 24, as said below
Outputs:
- ffn_out: bfloat16 [256, 8192], P(('groups', 'row', 'rep'), 'col'), parts along dimension 0
There are 2 independent parts, one for each index of `groups`. A program takes and returns all parts, laid end to end along the dimension named above; an argument that names none is the same for every part. Nothing has to cross between parts.
Inputs may be any that keep to these rules, and one draw needn't show every extreme that they name: `gate_cols`: each entry names a block column inside its panel; the 24 entries of one list are distinct. `gate_count`: slots below the count are live, later ones are padding; in every panel some block row has all 24 slots live. `up_cols`: each entry names a block column inside its panel; the 24 entries of one list are distinct. `up_count`: slots below the count are live, later ones are padding; in every panel some block row has all 24 slots live. `down_cols`: each entry names a block column inside its panel; the 24 entries of one list are distinct. `down_count`: slots below the count are live, later ones are padding; in every panel some block row has all 24 slots live.
All inputs are finite; a program needn't handle non-finite values.
Results may differ from a plain program's by a relative error of at most 0.0049.
Values may be sent and summed in bfloat16 or wider, within the bound.
A program may use at most 320 MiB of HBM per device.

v0:
```python
import jax
import jax.numpy as jnp
from jax import lax
from jax.sharding import PartitionSpec as P


def live_table(col_ids, live_count, width, kind):
    slots_here = col_ids.shape[2]
    slot_index = jnp.arange(slots_here, dtype=jnp.int32)
    is_live = slot_index[None, :] < live_count
    matches = col_ids[:, 0, :, None] == jnp.arange(width, dtype=jnp.int32)[None, None, :]
    return (matches & is_live[:, :, None]).astype(kind)


def dense_tile(blocks, col_ids, live_count, width):
    table = live_table(col_ids, live_count, width, jnp.bfloat16)
    spread = jnp.einsum("rsw,rsij->riwj", table, blocks[:, 0], preferred_element_type=jnp.float32)
    return spread.astype(jnp.bfloat16).reshape(
        blocks.shape[0] * blocks.shape[3], width * blocks.shape[4]
    )


def per_device(
    tokens,
    gate_blocks,
    gate_cols,
    gate_count,
    up_blocks,
    up_cols,
    up_count,
    down_blocks,
    down_cols,
    down_count,
):
    panel_width = down_blocks.shape[0]
    down_width = gate_blocks.shape[0]
    hidden_cols = panel_width * down_blocks.shape[3]
    both_tile = jnp.concatenate(
        (
            dense_tile(gate_blocks, gate_cols, gate_count, panel_width),
            dense_tile(up_blocks, up_cols, up_count, panel_width),
        ),
        axis=1,
    )
    down_tile = dense_tile(down_blocks, down_cols, down_count, down_width)
    partial_sums = jnp.dot(
        lax.all_gather(tokens, "row", axis=0, tiled=True),
        both_tile,
        preferred_element_type=jnp.float32,
    )
    totals = lax.psum(partial_sums, "col")
    hidden = (jax.nn.silu(totals[:, :hidden_cols]) * totals[:, hidden_cols:]).astype(jnp.bfloat16)
    result = lax.psum_scatter(
        jnp.dot(hidden, down_tile, preferred_element_type=jnp.float32),
        "row",
        scatter_dimension=0,
        tiled=True,
    )
    return result.astype(jnp.bfloat16)


def solution(mesh):
    return jax.shard_map(
        per_device,
        mesh=mesh,
        in_specs=(
            P(("groups", "row", "rep"), "col"),
            P("col", "row", None, None, None),
            P("col", "row", None),
            P("col", "row"),
            P("col", "row", None, None, None),
            P("col", "row", None),
            P("col", "row"),
            P("row", "col", None, None, None),
            P("row", "col", None),
            P("row", "col"),
        ),
        out_specs=P(("groups", "row", "rep"), "col"),
        check_vma=False,
    )
```

profile of v0, /device:TPU:0, one launch (start us, length us, event | category | flops | bytes accessed | tf_op | source)
XLA Modules:
  0.0 312.3 jit_solution(8671177271869001280)
XLA Ops:
  6.5 0.0 all-reduce.2.cloned.1.call-start
  6.5 0.8 copy.11
  7.3 0.7 iota_compare_fusion.5
  8.0 0.8 copy.13
  8.8 0.7 iota_compare_fusion.4
  9.6 17.6 %all_gather.3 = bf16[64,4096]{1,0:T(8,128)(2,1)S(1)} all-gather(bf16[16,4096]{1,0:T(8,128)(2,1)} %param.10), channel_id=1, replica_groups=mesh['groups'=2,'row'=4,'col'=2,'rep'=2] {'row'}, dimensions={0}, use_global_device_ids=true | all-gather | bytes 655360 | tf_op jit(solution)/shard_map/all_gather | solution.py:47
  27.1 30.5 %fusion.13 = bf16[32,32,128,128]{3,1,2,0:T(8,128)(2,1)} fusion(bf16[32,24,128,128]{3,2,1,0:T(8,128)(2,1)} %bitcast.46, s32[32,24]{1,0:T(8,128)S(1)} %copy.11, pred[32,24]{1,0:T(8,128)(4,1)S(1)} %iota_compare_fusion.5), kind=kOutput, calls=%fused_computation.15 | convolution fusion | flops 822132736 | bytes 58724096 | tf_op jit(solution)/shard_map/rsw,rsij->riwj/dot_general | solution.py:17
  57.6 30.6 %fusion.16 = bf16[32,32,128,128]{3,1,2,0:T(8,128)(2,1)} fusion(bf16[32,24,128,128]{3,2,1,0:T(8,128)(2,1)} %bitcast.47, s32[32,24]{1,0:T(8,128)S(1)} %copy.13, pred[32,24]{1,0:T(8,128)(4,1)S(1)} %iota_compare_fusion.4), kind=kOutput, calls=%fused_computation.16 | convolution fusion | flops 822132736 | bytes 58724096 | tf_op jit(solution)/shard_map/rsw,rsij->riwj/dot_general | solution.py:17
  88.2 77.2 %copy_bitcast_fusion = (bf16[4096,4096]{1,0:T(8,128)(2,1)}, bf16[4096,4096]{1,0:T(8,128)(2,1)}) fusion(bf16[512,8,32,128]{3,2,1,0:T(8,128)(2,1)} %bitcast.44, bf16[512,8,32,128]{3,2,1,0:T(8,128)(2,1)} %bitcast.43), kind=kLoop, calls=%fused_computation.7 | loop fusion | bytes 134217728 | tf_op jit(solution)/shard_map/reshape | solution.py:18
  165.5 0.0 copy-start
  165.5 0.0 copy-start.1
  165.5 24.4 %fusion.22 = f32[64,8192]{1,0:T(8,128)} fusion(bf16[64,4096]{1,0:T(8,128)(2,1)S(1)} %all_gather.3, bf16[4096,4096]{1,0:T(8,128)(2,1)} %get-tuple-element.5, bf16[4096,4096]{1,0:T(8,128)(2,1)} %get-tuple-element.6), kind=kOutput, calls=%fused_computation.18 | convolution fusion | flops 4429185024 | bytes 69730304 | tf_op jit(solution)/shard_map/dot_general | solution.py:46
  189.9 0.0 all-reduce.2.cloned.1.call-update
  189.9 0.0 reduce-scatter.2.cloned.1.call-start
  189.9 0.0 copy-done
  190.0 0.1 copy.15
  190.0 0.0 copy-done.1
  190.0 0.1 iota_compare_fusion.3
  190.1 30.5 %fusion.19 = bf16[32,32,128,128]{3,1,2,0:T(8,128)(2,1)} fusion(bf16[32,24,128,128]{3,2,1,0:T(8,128)(2,1)} %bitcast.48, s32[32,24]{1,0:T(8,128)S(1)} %copy.15, pred[32,24]{1,0:T(8,128)(4,1)S(1)} %iota_compare_fusion.3), kind=kOutput, calls=%fused_computation.17 | convolution fusion | flops 822132736 | bytes 58724096 | tf_op jit(solution)/shard_map/rsw,rsij->riwj/dot_general | solution.py:17
  220.6 34.1 %all-reduce.2.cloned.1.call-done = f32[64,8192]{1,0:T(8,128)} async-done(((f32[64,8192]{1,0:T(8,128)}), f32[64,8192]{1,0:T(8,128)}) %all-reduce.2.cloned.1.call-update) | async-done | bytes 2097168 | tf_op jit(solution)/shard_map/psum | solution.py:51
  254.7 21.8 %fusion.4 = f32[64,4096]{1,0:T(8,128)} fusion(bf16[512,8,32,128]{3,2,1,0:T(8,128)(2,1)} %bitcast.45, f32[64,8192]{1,0:T(8,128)} %all-reduce.2.cloned.1.call-done), kind=kOutput, calls=%fused_computation.4 | convolution fusion | flops 2149056512 | bytes 36700160 | tf_op jit(solution)/shard_map/dot_general | solution.py:54
  276.5 0.0 reduce-scatter.2.cloned.1.call-update
  276.5 27.3 %reduce-scatter.2.cloned.1.call-done = f32[16,4096]{1,0:T(8,128)} async-done(((f32[64,4096]{1,0:T(8,128)}), f32[16,4096]{1,0:T(8,128)}) %reduce-scatter.2.cloned.1.call-update) | async-done | bytes 262160 | tf_op jit(solution)/shard_map/reduce_scatter | solution.py:53
  303.8 1.6 convert_element_type.34
Async XLA Ops:
  6.5 248.2 %all-reduce.2.cloned.1.call-start = ((), (), s32[]{:S(2)}) async-start(), calls=%async_computation.1 | async-start | bytes 4194304 | tf_op jit(solution)/shard_map/psum | solution.py:51
  165.5 24.5 %copy-start = (s32[32,1,24]{0,2,1:T(8,128)S(1)}, s32[32,1,24]{0,2,1:T(8,128)}, u32[]{:S(2)}) copy-start(s32[32,1,24]{0,2,1:T(8,128)} %param.18) | copy-start | bytes 9220
  165.5 24.6 %copy-start.1 = (s32[32,1]{0,1:T(1,128)S(1)}, s32[32,1]{0,1:T(1,128)}, u32[]{:S(2)}) copy-start(s32[32,1]{0,1:T(1,128)} %param.19) | copy-start | bytes 388
  189.9 113.9 %reduce-scatter.2.cloned.1.call-start = ((), (), s32[]{:S(2)}) async-start(), calls=%async_computation.2 | async-start | bytes 1310720 | tf_op jit(solution)/shard_map/reduce_scatter | solution.py:53
Sparse Core Ops, SparseCore 0:
  190.0 64.6 all-reduce.1
  276.6 27.1 reduce-scatter.1
where the time goes:
time: 313 us; the launch traced here: 312 us
  matrix products  138 us (44%)
  local copies, waits for them, and re-layouts  78.9 us (25%)
  waiting for transfers between devices  61.4 us (20%)
  blocking collectives  17.6 us (6%)
  between operations  13.4 us (4%)
  other arithmetic  3.15 us (1%)
    dot_general x3, matrix products, dense_tile(): jnp.einsum('rsw,rsij->riwj', table, blocks[:, 0], preferred_element_type=...  91.6 us
    reshape x1, local copies, waits for them, and re-layouts, dense_tile(): spread.astype(jnp.bfloat16)  77.2 us
    psum x1, waiting for transfers between devices, per_device(): totals = lax.psum(partial_sums, 'col')  34.1 us
    reduce_scatter x1, waiting for transfers between devices, per_device(): lax.psum_scatter(jnp.dot(hidden, down_tile, preferred_element_type=jnp.fl...  27.3 us
    dot_general x1, matrix products, per_device(): jnp.dot(lax.all_gather(tokens, 'row', axis=0, tiled=True), both_tile, pre...  24.4 us
    dot_general x1, matrix products, per_device(): jnp.dot(hidden, down_tile, preferred_element_type=jnp.float32)  21.8 us
    all_gather x1, blocking collectives, per_device(): lax.all_gather(tokens, 'row', axis=0, tiled=True)  17.6 us
  transfers between devices with their start and end apart: 2, of which 2 were waited for; matrix products, arithmetic and copies ran while one was open for 10% of the time, Pallas kernels for 0%

commit v1 on v0

v1 whole, which is shorter than its diff:
```python
import functools

import jax
import jax.numpy as jnp
from jax import lax
from jax.experimental import pallas as pl
from jax.experimental.pallas import tpu as pltpu
from jax.sharding import PartitionSpec as P

BF = jnp.bfloat16
F32 = jnp.float32
MESH = pl.DeviceIdType.MESH


def live_table(col_ids, live_count, width, kind):
    slots_here = col_ids.shape[2]
    slot_index = jnp.arange(slots_here, dtype=jnp.int32)
    is_live = slot_index[None, :] < live_count
    matches = col_ids[:, 0, :, None] == jnp.arange(width, dtype=jnp.int32)[None, None, :]
    return (matches & is_live[:, :, None]).astype(kind)


def dense_tile(blocks, col_ids, live_count, width):
    table = live_table(col_ids, live_count, width, BF)
    spread = jnp.einsum("rsw,rsij->riwj", table, blocks[:, 0], preferred_element_type=F32)
    return spread.astype(BF).reshape(blocks.shape[0] * blocks.shape[3], width * blocks.shape[4])


def general(tokens, gate_blocks, gate_cols, gate_count, up_blocks, up_cols, up_count,
            down_blocks, down_cols, down_count):
    panel_width = down_blocks.shape[0]
    down_width = gate_blocks.shape[0]
    hidden_cols = panel_width * down_blocks.shape[3]
    both_tile = jnp.concatenate(
        (
            dense_tile(gate_blocks, gate_cols, gate_count, panel_width),
            dense_tile(up_blocks, up_cols, up_count, panel_width),
        ),
        axis=1,
    )
    down_tile = dense_tile(down_blocks, down_cols, down_count, down_width)
    partial_sums = jnp.dot(
        lax.all_gather(tokens, "row", axis=0, tiled=True), both_tile, preferred_element_type=F32
    )
    totals = lax.psum(partial_sums, "col")
    hidden = (jax.nn.silu(totals[:, :hidden_cols]) * totals[:, hidden_cols:]).astype(BF)
    result = lax.psum_scatter(
        jnp.dot(hidden, down_tile, preferred_element_type=F32),
        "row", scatter_dimension=0, tiled=True,
    )
    return result.astype(BF)


CH = 4


def slot_table(col_ids, live_count, width):
    slots = col_ids.shape[2]
    slot = jnp.arange(slots, dtype=jnp.int32)
    live = slot[None, :] < live_count
    hit = (col_ids[:, 0, None, :] == jnp.arange(width, dtype=jnp.int32)[None, :, None]) & live[:, None, :]
    return slots + jnp.sum(jnp.where(hit, slot - slots, 0), axis=2)


def kernel(n_row, tok_ref, g_hbm, u_hbm, d_hbm, tab, out_ref,
           wg, wu, wd, tokbuf, ssend, srecv, xsend, xrecv, own, hid, dsend, drecv, dacc, zsend, zrecv,
           wsem, lsem, tok_s, tok_r, sib_s, sib_r, x_s, x_r, h_s, h_r, d_s, d_r, z_s, z_r):
    r = lax.axis_index("row")
    c = lax.axis_index("col")
    p = lax.axis_index("rep")
    nc, np_ = 1 - c, 1 - p
    rows, slots = wg.shape[0], wg.shape[1] - 1
    drows = wd.shape[0]
    blk = wg.shape[2]
    g_rows = g_hbm.shape[0]
    t = tok_ref.shape[0]
    kh = tokbuf.shape[2]
    n_tok = tokbuf.shape[0] * t
    half = n_row * t
    hb = drows
    qb = hb // 2
    pairs = qb // 2
    per = pairs // CH
    step = 2 * blk

    loads = []
    for n, (w, src, nr) in enumerate(((wg, g_hbm, rows), (wu, u_hbm, rows), (wd, d_hbm, drows))):
        w[:, slots] = jnp.zeros((nr, blk, blk), BF)
        for q in range(2):
            hr = nr // 2
            cp = pltpu.make_async_copy(
                src.at[pl.ds(p * nr + q * hr, hr)],
                w.at[pl.ds(q * hr, hr), pl.ds(0, slots)],
                wsem.at[n, q],
            )
            cp.start()
            loads.append(cp)

    peers = [(k, e) for k in range(n_row) for e in range(2) if (k, e) != (0, 0)]

    def peer(k, e):
        return {"row": lax.rem(r + k, n_row), "rep": lax.rem(p + e, 2)}

    barrier = pltpu.get_barrier_semaphore()
    for k, e in peers:
        pl.semaphore_signal(barrier, inc=1, device_id=peer(k, e), device_id_type=MESH)
    pl.semaphore_signal(barrier, inc=1, device_id={"col": nc}, device_id_type=MESH)
    pl.semaphore_wait(barrier, len(peers) + 1)

    me = p * n_row + r
    toks = []
    for k, e in sorted(peers, key=lambda ke: -ke[0]):
        pe = lax.rem(p + e, 2)
        cp = pltpu.make_async_remote_copy(
            src_ref=tok_ref.at[:, pl.ds(pl.multiple_of(pe * kh, 128), kh)],
            dst_ref=tokbuf.at[me],
            send_sem=tok_s.at[k * 2 + e], recv_sem=tok_r.at[k * 2 + e],
            device_id=peer(k, e), device_id_type=MESH,
        )
        cp.start()
        toks.append(cp)
    mine = pltpu.make_async_copy(
        tok_ref.at[:, pl.ds(pl.multiple_of(p * kh, 128), kh)], tokbuf.at[me], lsem.at[0])
    mine.start()
    mine.wait()
    for cp in loads[:4]:
        cp.wait()
    for cp in toks:
        cp.wait_recv()

    def product(x_of, w, base, nr, j):
        total = None
        for i in range(0, nr, 2):
            w2 = jnp.concatenate(
                [jnp.concatenate([w[a, tab[base + a, j + b]] for b in range(2)], axis=1) for a in (i, i + 1)],
                axis=0,
            )
            term = jnp.dot(x_of(i), w2, preferred_element_type=F32)
            total = term if total is None else total + term
        return total

    def tok_at(i):
        return tokbuf[:, :, i * blk:(i + 2) * blk].reshape(n_tok, step)

    def both(j):
        return (product(tok_at, wg, p * rows, rows, j),
                product(tok_at, wu, g_rows + p * rows, rows, j))

    def to_sibling(n):
        return pltpu.make_async_remote_copy(
            src_ref=ssend.at[n], dst_ref=srecv.at[n], send_sem=sib_s.at[n], recv_sem=sib_r.at[n],
            device_id={"rep": np_}, device_id_type=MESH)

    def to_col(u):
        return pltpu.make_async_remote_copy(
            src_ref=xsend.at[u], dst_ref=xrecv.at[u], send_sem=x_s.at[u], recv_sem=x_r.at[u],
            device_id={"col": nc}, device_id_type=MESH)

    def hid_copy(u):
        return pltpu.make_async_remote_copy(
            src_ref=hid.at[c * CH + u], dst_ref=hid.at[c * CH + u], send_sem=h_s.at[u], recv_sem=h_r.at[u],
            device_id={"col": nc}, device_id_type=MESH)

    cw = step * per

    def sib_part(h, quarter):
        def body(u, _):
            for v in range(per):
                gate, up = both(np_ * hb + quarter * qb + 2 * (u * per + v))
                ssend[h * CH + u, :, v * step:(v + 1) * step] = gate.astype(BF)
                ssend[h * CH + u, :, cw + v * step:cw + (v + 1) * step] = up.astype(BF)
            to_sibling(h * CH + u).start()
            return 0
        lax.fori_loop(0, CH, body, 0)

    def own_part(u, quarter):
        for v in range(per):
            gate, up = both(p * hb + quarter * qb + 2 * (u * per + v))
            own[u, :, v * step:(v + 1) * step] = gate
            own[u, :, cw + v * step:cw + (v + 1) * step] = up

    sib_part(0, nc)

    def col_body(u, _):
        own_part(u, nc)
        to_sibling(u).wait_recv()
        xsend[u] = (own[u] + srecv[u].astype(F32)).astype(BF)
        to_col(u).start()
        return 0

    lax.fori_loop(0, CH, col_body, 0)
    sib_part(1, c)

    def keep_body(u, _):
        own_part(u, c)
        return 0

    lax.fori_loop(0, CH, keep_body, 0)

    def hid_body(u, _):
        to_sibling(CH + u).wait_recv()
        to_col(u).wait_recv()
        tot = own[u] + srecv[CH + u].astype(F32) + xrecv[u].astype(F32)
        gate, up = tot[:, :cw], tot[:, cw:]
        hid[c * CH + u] = (gate / (1.0 + jnp.exp(-gate)) * up).astype(BF)
        hid_copy(u).start()
        return 0

    lax.fori_loop(0, CH, hid_body, 0)
    for cp in loads[4:]:
        cp.wait()
    for u in range(CH):
        hid_copy(u).wait_recv()

    def hid_at(i):
        n, at = divmod(i * blk, cw)
        return hid[n, :, at:at + step]

    oc = dacc.shape[2]
    opairs = oc // step

    def d_copy(ch):
        return pltpu.make_async_remote_copy(
            src_ref=dsend.at[ch], dst_ref=drecv.at[ch], send_sem=d_s.at[ch], recv_sem=d_r.at[ch],
            device_id={"rep": np_}, device_id_type=MESH)

    def z_copy(ch, k):
        to = lax.rem(r + k, n_row)
        return pltpu.make_async_remote_copy(
            src_ref=zsend.at[ch, pl.ds(pl.multiple_of(to * t, t), t)], dst_ref=zrecv.at[ch, k - 1],
            send_sem=z_s.at[ch, k - 1], recv_sem=z_r.at[ch, k - 1],
            device_id={"row": to}, device_id_type=MESH)

    def z_part(ch):
        d_copy(ch).wait_recv()
        tot = dacc[ch] + drecv[ch].astype(F32)
        dacc[ch] = tot
        zsend[ch] = tot.astype(BF)
        for k in range(n_row - 1, 0, -1):
            z_copy(ch, k).start()

    keep_at = pl.multiple_of(p * half, half)
    give_at = pl.multiple_of(np_ * half, half)

    for ch in range(CH):
        def down_body(v, _):
            res = product(hid_at, wd, 2 * g_rows + p * drows, drows, (ch * opairs + v) * 2)
            at = pl.multiple_of(v * step, step)
            lo, hi = res[:half], res[half:]
            first = (p == 0)
            dacc[ch, :, pl.ds(at, step)] = jnp.where(first, lo, hi)
            dsend[ch, :, pl.ds(at, step)] = jnp.where(first, hi, lo).astype(BF)
            return 0
        lax.fori_loop(0, opairs, down_body, 0)
        d_copy(ch).start()
        if ch:
            z_part(ch - 1)
    z_part(CH - 1)

    for ch in range(CH):
        tot = dacc[ch, pl.ds(pl.multiple_of(r * t, t), t), :]
        for k in range(1, n_row):
            z_copy(ch, k).wait_recv()
            tot = tot + zrecv[ch, k - 1].astype(F32)
        out_ref[:, ch * oc:(ch + 1) * oc] = tot.astype(BF)

    for cp in toks:
        cp.wait_send()
    for n in range(2 * CH):
        to_sibling(n).wait_send()
    for u in range(CH):
        to_col(u).wait_send()
        hid_copy(u).wait_send()
        d_copy(u).wait_send()
        for k in range(1, n_row):
            z_copy(u, k).wait_send()


def fused(n_row, tokens, gate_blocks, gate_cols, gate_count, up_blocks, up_cols, up_count,
          down_blocks, down_cols, down_count):
    t, kc = tokens.shape
    g_rows, _, slots, blk, _ = gate_blocks.shape
    d_rows = down_blocks.shape[0]
    table = jnp.concatenate(
        (
            slot_table(gate_cols, gate_count, d_rows),
            slot_table(up_cols, up_count, d_rows),
            slot_table(down_cols, down_count, g_rows),
        ),
        axis=0,
    )
    rows, drows = g_rows // 2, d_rows // 2
    n_tok = n_row * 2 * t
    half = n_row * t
    cw = drows * blk // 2 // CH
    oc = kc // CH
    V = pltpu.VMEM
    dma = pltpu.SemaphoreType.DMA
    return pl.pallas_call(
        functools.partial(kernel, n_row),
        out_shape=jax.ShapeDtypeStruct((t, kc), BF),
        in_specs=[pl.BlockSpec(memory_space=pltpu.VMEM)]
        + [pl.BlockSpec(memory_space=pl.ANY)] * 3
        + [pl.BlockSpec(memory_space=pltpu.SMEM)],
        out_specs=pl.BlockSpec(memory_space=pltpu.VMEM),
        scratch_shapes=[
            V((rows, slots + 1, blk, blk), BF),
            V((rows, slots + 1, blk, blk), BF),
            V((drows, slots + 1, blk, blk), BF),
            V((n_row * 2, t, kc // 2), BF),
            V((2 * CH, n_tok, 2 * cw), BF),
            V((2 * CH, n_tok, 2 * cw), BF),
            V((CH, n_tok, 2 * cw), BF),
            V((CH, n_tok, 2 * cw), BF),
            V((CH, n_tok, 2 * cw), F32),
            V((2 * CH, n_tok, cw), BF),
            V((CH, half, oc), BF),
            V((CH, half, oc), BF),
            V((CH, half, oc), F32),
            V((CH, half, oc), BF),
            V((CH, n_row - 1, t, oc), BF),
            dma((3, 2)),
            dma((1,)),
            dma((2 * n_row,)), dma((2 * n_row,)),
            dma((2 * CH,)), dma((2 * CH,)),
            dma((CH,)), dma((CH,)),
            dma((CH,)), dma((CH,)),
            dma((CH,)), dma((CH,)),
            dma((CH, n_row - 1)), dma((CH, n_row - 1)),
        ],
        compiler_params=pltpu.CompilerParams(
            collective_id=0, has_side_effects=True, vmem_limit_bytes=60 * 2**20),
        cost_estimate=pl.CostEstimate(
            flops=2 * n_tok * (2 * rows * d_rows + drows * g_rows) * blk * blk,
            bytes_accessed=2 * (2 * rows + drows) * slots * blk * blk,
            transcendentals=n_tok * cw * CH),
    )(tokens, gate_blocks[:, 0], up_blocks[:, 0], down_blocks[:, 0], table)


def fits(mesh, n_tok, gate_blocks, down_blocks):
    rows, slots = gate_blocks.shape[0], gate_blocks.shape[2]
    weights = (rows * (slots + 1) + down_blocks.shape[0] * (slots + 1) // 2) * gate_blocks.shape[3] ** 2 * 2
    return (mesh.shape["col"] == 2 and mesh.shape["rep"] == 2 and n_tok <= 128
            and slots == down_blocks.shape[2] and gate_blocks.shape[0] == down_blocks.shape[0]
            and rows % 4 == 0 and down_blocks.shape[0] % (8 * CH) == 0 and weights <= 40 * 2**20)


def solution(mesh):
    n_row = mesh.shape["row"]

    def per_device(tokens, *rest):
        if fits(mesh, n_row * 2 * tokens.shape[0], rest[0], rest[6]):
            return fused(n_row, tokens, *rest)
        return general(tokens, *rest)

    return jax.shard_map(
        per_device,
        mesh=mesh,
        in_specs=(
            P(("groups", "row", "rep"), "col"),
            P("col", "row", None, None, None),
            P("col", "row", None),
            P("col", "row"),
            P("col", "row", None, None, None),
            P("col", "row", None),
            P("col", "row"),
            P("row", "col", None, None, None),
            P("row", "col", None),
            P("row", "col"),
        ),
        out_specs=P(("groups", "row", "rep"), "col"),
        check_vma=False,
    )
```

time: 313 us -> 65.9 us (0.21)
  matrix products: 138 us -> 0 us
  local copies, waits for them, and re-layouts: 78.9 us -> 3.91 us
  waiting for transfers between devices: 61.4 us -> 0 us
  Pallas kernels: 0 us -> 57.9 us
  blocking collectives: 17.6 us -> 0 us
  between operations: 13.4 us -> 0.04 us
    dot_general x5 -> x0, matrix products: 138 us -> none  [the longest x3 91.6 us: dense_tile(): jnp.einsum('rsw,rsij->riwj', table, blocks[:, 0], preferred_element_type=...]
    reshape x1 -> x0, local copies, waits for them, and re-layouts: 77.2 us -> none  [dense_tile(): spread.astype(jnp.bfloat16)]
    pallas_call x0 -> x1, Pallas kernels: none -> 57.9 us  [fused(): pl.pallas_call(functools.partial(kernel, n_row), out_shape=jax.ShapeDtype...]
    psum x1 -> x0, waiting for transfers between devices: 34.1 us -> none  [per_device(): totals = lax.psum(partial_sums, 'col')]
    reduce_scatter x1 -> x0, waiting for transfers between devices: 27.3 us -> none  [per_device(): lax.psum_scatter(jnp.dot(hidden, down_tile, preferred_element_type=jnp.fl...]
    all_gather x1 -> x0, blocking collectives: 17.6 us -> none  [per_device(): lax.all_gather(tokens, 'row', axis=0, tiled=True)]
  transfers between devices with their start and end apart: 2 -> 0, of which waited for: 2 -> 0; matrix products, arithmetic and copies ran while one was open for 10% -> 0% of each run, Pallas kernels for 0% -> 0%
where the time goes in v1:
time: 65.9 us; the launch traced here: 65.5 us
  Pallas kernels  57.9 us (88%)
  local copies, waits for them, and re-layouts  3.91 us (6%)
  other arithmetic  3.71 us (6%)
    pallas_call x1, Pallas kernels, fused(): pl.pallas_call(functools.partial(kernel, n_row), out_shape=jax.ShapeDtype...  57.9 us
    eq x3, local copies, waits for them, and re-layouts, slot_table(): col_ids[:, 0, None, :] == jnp.arange(width, dtype=jnp.int32)[None, :, None]  2.34 us
    lt x3, other arithmetic, slot_table(): live = slot[None, :] < live_count  2.18 us
    unnamed x1, local copies, waits for them, and re-layouts  1.57 us

profile of v1, /device:TPU:0, one launch (start us, length us, event | category | flops | bytes accessed | tf_op | source)
XLA Modules:
  0.0 65.5 jit_solution(17303551680306370923)
XLA Ops:
  0.0 0.7 %iota_compare_fusion.5 = pred[32,24]{1,0:T(8,128)(4,1)S(1)} fusion(s32[32]{0:T(128)} %bitcast.15), kind=kLoop, calls=%fused_computation.12 | loop fusion | flops 768 | bytes 896 | tf_op jit(solution)/shard_map/lt | solution.py:60
  0.7 0.7 %iota_compare_fusion.4 = pred[32,24]{1,0:T(8,128)(4,1)S(1)} fusion(s32[32]{0:T(128)} %bitcast.16), kind=kLoop, calls=%fused_computation.11 | loop fusion | flops 768 | bytes 896 | tf_op jit(solution)/shard_map/lt | solution.py:60
  1.5 0.7 %iota_compare_fusion.3 = pred[32,24]{1,0:T(8,128)(4,1)S(1)} fusion(s32[32]{0:T(128)} %bitcast.17), kind=kLoop, calls=%fused_computation.10 | loop fusion | flops 768 | bytes 896 | tf_op jit(solution)/shard_map/lt | solution.py:60
  2.2 0.8 %copy.25 = s32[32,24]{1,0:T(8,128)S(1)} copy(s32[32,24]{0,1:T(8,128)} %bitcast.12) | data formatting | bytes 6144 | tf_op jit(solution)/shard_map/eq | solution.py:61
  3.0 0.8 %copy.26 = s32[32,24]{1,0:T(8,128)S(1)} copy(s32[32,24]{0,1:T(8,128)} %bitcast.13) | data formatting | bytes 6144 | tf_op jit(solution)/shard_map/eq | solution.py:61
  3.8 0.8 %copy.27 = s32[32,24]{1,0:T(8,128)S(1)} copy(s32[32,24]{0,1:T(8,128)} %bitcast.14) | data formatting | bytes 6144 | tf_op jit(solution)/shard_map/eq | solution.py:61
  4.5 0.9 %select_reduce_fusion.2 = (s32[32,32]{1,0:T(8,128)S(1)}, s32[32,32]{1,0:T(8,128)S(1)}, s32[32,32]{1,0:T(8,128)S(1)}) fusion(s32[24]{0:T(128)S(1)} %iota_add_fusion, s32[32,24]{1,0:T(8,128)S(1)} %copy.25, pred[32,24]{1,0:T(8,128)(4,1)S(1)} %iota_compare_fusion.5, pred[32,24]{1,0:T(8,128)(4,1)S(1)} %iota_compare_fusion.4, s32[32,24]{1,0:T(8,128)S(1)} %copy.26, ...), kind=kLoop, calls=%fused_computation.4 | loop fusion | flops 291840 | bytes 23904 | tf_op jit(solution)/shard_map/reduce_sum | solution.py:62
  5.5 0.6 pad_add_fusion.tab
  6.1 57.9 %shard_map.100 = bf16[16,4096]{1,0:T(8,128)(2,1)} custom-call(bf16[16,4096]{1,0:T(8,128)(2,1)} %tok_ref.1, bf16[32,24,128,128]{3,2,1,0:T(8,128)(2,1)} %bitcast.9, bf16[32,24,128,128]{3,2,1,0:T(8,128)(2,1)} %bitcast.10, bf16[32,24,128,128]{3,2,1,0:T(8,128)(2,1)} %bitcast.11, s32[96,32]{1,0:T(8,128)} %pad_add_fusion.tab), custom_call_target="tpu_custom_call" | custom-call | flops 6442450944 | bytes 37748736 | tf_op jit(solution)/shard_map/pallas_call | solution.py:299
  63.9 1.6 %copy.29 = bf16[16,4096]{1,0:T(8,128)(2,1)} copy(bf16[16,4096]{1,0:T(8,128)(2,1)} %shard_map.100) | data formatting | bytes 262144
  (3 shorter events, 0.0 us)

commit v2 on v1

--- a/solution.py
+++ b/solution.py
@@ -54,16 +54,18 @@
 CH = 4
 
 
-def slot_table(col_ids, live_count, width):
-    slots = col_ids.shape[2]
-    slot = jnp.arange(slots, dtype=jnp.int32)
-    live = slot[None, :] < live_count
-    hit = (col_ids[:, 0, None, :] == jnp.arange(width, dtype=jnp.int32)[None, :, None]) & live[:, None, :]
-    return slots + jnp.sum(jnp.where(hit, slot - slots, 0), axis=2)
-
-
-def kernel(n_row, tok_ref, g_hbm, u_hbm, d_hbm, tab, out_ref,
-           wg, wu, wd, tokbuf, ssend, srecv, xsend, xrecv, own, hid, dsend, drecv, dacc, zsend, zrecv,
+def slot_table(cols_ref, count_ref, width):
+    slots, block_rows = cols_ref.shape
+    count = count_ref[...]
+    column = lax.broadcasted_iota(jnp.int32, (width, block_rows), 0)
+    found = jnp.full(column.shape, slots, jnp.int32)
+    for s in range(slots):
+        found = jnp.where((cols_ref[s:s + 1, :] == column) & (count > s), s, found)
+    return found
+
+
+def kernel(n_row, tok_ref, g_hbm, u_hbm, d_hbm, gc_ref, gn_ref, uc_ref, un_ref, dc_ref, dn_ref, out_ref,
+           tabv, tab, dfull, wg, wu, wd, tokbuf, ssend, srecv, xsend, xrecv, own, hid, dsend, drecv, dacc, zsend, zrecv,
            wsem, lsem, tok_s, tok_r, sib_s, sib_r, x_s, x_r, h_s, h_r, d_s, d_r, z_s, z_r):
     r = lax.axis_index("row")
     c = lax.axis_index("col")
@@ -72,7 +74,7 @@
     rows, slots = wg.shape[0], wg.shape[1] - 1
     drows = wd.shape[0]
     blk = wg.shape[2]
-    g_rows = g_hbm.shape[0]
+    width = tabv.shape[0] // 3
     t = tok_ref.shape[0]
     kh = tokbuf.shape[2]
     n_tok = tokbuf.shape[0] * t
@@ -122,17 +124,24 @@
     mine = pltpu.make_async_copy(
         tok_ref.at[:, pl.ds(pl.multiple_of(p * kh, 128), kh)], tokbuf.at[me], lsem.at[0])
     mine.start()
+    tabv[...] = jnp.zeros_like(tabv)
+    for n, (cr, cn) in enumerate(((gc_ref, gn_ref), (uc_ref, un_ref), (dc_ref, dn_ref))):
+        tabv[n * width:(n + 1) * width, :cr.shape[1]] = slot_table(cr, cn, width)
+    table = pltpu.make_async_copy(tabv, tab, lsem.at[1])
+    table.start()
+    dfull[...] = jnp.zeros_like(dfull)
     mine.wait()
+    table.wait()
     for cp in loads[:4]:
         cp.wait()
     for cp in toks:
         cp.wait_recv()
 
-    def product(x_of, w, base, nr, j):
+    def product(x_of, w, at, row0, nr, j):
         total = None
         for i in range(0, nr, 2):
             w2 = jnp.concatenate(
-                [jnp.concatenate([w[a, tab[base + a, j + b]] for b in range(2)], axis=1) for a in (i, i + 1)],
+                [jnp.concatenate([w[a, tab[at + j + b, row0 + a]] for b in range(2)], axis=1) for a in (i, i + 1)],
                 axis=0,
             )
             term = jnp.dot(x_of(i), w2, preferred_element_type=F32)
@@ -143,8 +152,8 @@
         return tokbuf[:, :, i * blk:(i + 2) * blk].reshape(n_tok, step)
 
     def both(j):
-        return (product(tok_at, wg, p * rows, rows, j),
-                product(tok_at, wu, g_rows + p * rows, rows, j))
+        return (product(tok_at, wg, 0, p * rows, rows, j),
+                product(tok_at, wu, width, p * rows, rows, j))
 
     def to_sibling(n):
         return pltpu.make_async_remote_copy(
@@ -167,8 +176,8 @@
         def body(u, _):
             for v in range(per):
                 gate, up = both(np_ * hb + quarter * qb + 2 * (u * per + v))
-                ssend[h * CH + u, :, v * step:(v + 1) * step] = gate.astype(BF)
-                ssend[h * CH + u, :, cw + v * step:cw + (v + 1) * step] = up.astype(BF)
+                ssend[h * CH + u, :, v * step:(v + 1) * step] = gate
+                ssend[h * CH + u, :, cw + v * step:cw + (v + 1) * step] = up
             to_sibling(h * CH + u).start()
             return 0
         lax.fori_loop(0, CH, body, 0)
@@ -184,7 +193,7 @@
     def col_body(u, _):
         own_part(u, nc)
         to_sibling(u).wait_recv()
-        xsend[u] = (own[u] + srecv[u].astype(F32)).astype(BF)
+        xsend[u] = (own[u] + srecv[u]).astype(BF)
         to_col(u).start()
         return 0
 
@@ -200,21 +209,51 @@
     def hid_body(u, _):
         to_sibling(CH + u).wait_recv()
         to_col(u).wait_recv()
-        tot = own[u] + srecv[CH + u].astype(F32) + xrecv[u].astype(F32)
+        tot = own[u] + srecv[CH + u] + xrecv[u].astype(F32)
         gate, up = tot[:, :cw], tot[:, cw:]
         hid[c * CH + u] = (gate / (1.0 + jnp.exp(-gate)) * up).astype(BF)
         hid_copy(u).start()
         return 0
 
-    lax.fori_loop(0, CH, hid_body, 0)
     for cp in loads[4:]:
         cp.wait()
-    for u in range(CH):
+    kc = dfull.shape[1]
+
+    def down_term(n, v):
+        total = None
+        for q in range(per):
+            row = (n * per + q) * 2
+            w2 = jnp.concatenate(
+                [jnp.concatenate(
+                    [wd[row + a, tab[2 * width + 2 * v + b, p * drows + row + a]] for b in range(2)], axis=1)
+                 for a in range(2)],
+                axis=0,
+            )
+            term = jnp.dot(hid[n, :, q * step:(q + 1) * step], w2, preferred_element_type=F32)
+            total = term if total is None else total + term
+        return total
+
+    def add_chunk(n):
+        def body(v, _):
+            at = pl.multiple_of(v * step, step)
+            dfull[:, pl.ds(at, step)] += down_term(n, v)
+            return 0
+        lax.fori_loop(0, kc // step, body, 0, unroll=4)
+
+    def own_body(u, _):
+        hid_body(u, 0)
+        add_chunk(c * CH + u)
+        return 0
+
+    lax.fori_loop(0, CH, own_body, 0)
+
+    def other_body(u, _):
         hid_copy(u).wait_recv()
-
-    def hid_at(i):
-        n, at = divmod(i * blk, cw)
-        return hid[n, :, at:at + step]
+        add_chunk(nc * CH + u)
+        return 0
+
+    lax.fori_loop(0, CH - 1, other_body, 0)
+    hid_copy(CH - 1).wait_recv()
 
     oc = dacc.shape[2]
     opairs = oc // step
@@ -233,23 +272,21 @@
 
     def z_part(ch):
         d_copy(ch).wait_recv()
-        tot = dacc[ch] + drecv[ch].astype(F32)
+        tot = dacc[ch] + drecv[ch]
         dacc[ch] = tot
         zsend[ch] = tot.astype(BF)
         for k in range(n_row - 1, 0, -1):
             z_copy(ch, k).start()
 
-    keep_at = pl.multiple_of(p * half, half)
-    give_at = pl.multiple_of(np_ * half, half)
-
     for ch in range(CH):
         def down_body(v, _):
-            res = product(hid_at, wd, 2 * g_rows + p * drows, drows, (ch * opairs + v) * 2)
             at = pl.multiple_of(v * step, step)
+            whole = pl.multiple_of(ch * oc + v * step, step)
+            res = dfull[:, pl.ds(whole, step)] + down_term(nc * CH + CH - 1, ch * opairs + v)
             lo, hi = res[:half], res[half:]
             first = (p == 0)
             dacc[ch, :, pl.ds(at, step)] = jnp.where(first, lo, hi)
-            dsend[ch, :, pl.ds(at, step)] = jnp.where(first, hi, lo).astype(BF)
+            dsend[ch, :, pl.ds(at, step)] = jnp.where(first, hi, lo)
             return 0
         lax.fori_loop(0, opairs, down_body, 0)
         d_copy(ch).start()
@@ -281,14 +318,6 @@
     t, kc = tokens.shape
     g_rows, _, slots, blk, _ = gate_blocks.shape
     d_rows = down_blocks.shape[0]
-    table = jnp.concatenate(
-        (
-            slot_table(gate_cols, gate_count, d_rows),
-            slot_table(up_cols, up_count, d_rows),
-            slot_table(down_cols, down_count, g_rows),
-        ),
-        axis=0,
-    )
     rows, drows = g_rows // 2, d_rows // 2
     n_tok = n_row * 2 * t
     half = n_row * t
@@ -301,26 +330,29 @@
         out_shape=jax.ShapeDtypeStruct((t, kc), BF),
         in_specs=[pl.BlockSpec(memory_space=pltpu.VMEM)]
         + [pl.BlockSpec(memory_space=pl.ANY)] * 3
-        + [pl.BlockSpec(memory_space=pltpu.SMEM)],
+        + [pl.BlockSpec(memory_space=pltpu.VMEM)] * 6,
         out_specs=pl.BlockSpec(memory_space=pltpu.VMEM),
         scratch_shapes=[
+            V((3 * d_rows, 128), jnp.int32),
+            pltpu.SMEM((3 * d_rows, 128), jnp.int32),
+            V((n_tok, kc), F32),
             V((rows, slots + 1, blk, blk), BF),
             V((rows, slots + 1, blk, blk), BF),
             V((drows, slots + 1, blk, blk), BF),
             V((n_row * 2, t, kc // 2), BF),
-            V((2 * CH, n_tok, 2 * cw), BF),
-            V((2 * CH, n_tok, 2 * cw), BF),
+            V((2 * CH, n_tok, 2 * cw), F32),
+            V((2 * CH, n_tok, 2 * cw), F32),
             V((CH, n_tok, 2 * cw), BF),
             V((CH, n_tok, 2 * cw), BF),
             V((CH, n_tok, 2 * cw), F32),
             V((2 * CH, n_tok, cw), BF),
-            V((CH, half, oc), BF),
-            V((CH, half, oc), BF),
+            V((CH, half, oc), F32),
+            V((CH, half, oc), F32),
             V((CH, half, oc), F32),
             V((CH, half, oc), BF),
             V((CH, n_row - 1, t, oc), BF),
             dma((3, 2)),
-            dma((1,)),
+            dma((2,)),
             dma((2 * n_row,)), dma((2 * n_row,)),
             dma((2 * CH,)), dma((2 * CH,)),
             dma((CH,)), dma((CH,)),
@@ -334,7 +366,8 @@
             flops=2 * n_tok * (2 * rows * d_rows + drows * g_rows) * blk * blk,
             bytes_accessed=2 * (2 * rows + drows) * slots * blk * blk,
             transcendentals=n_tok * cw * CH),
-    )(tokens, gate_blocks[:, 0], up_blocks[:, 0], down_blocks[:, 0], table)
+    )(tokens, gate_blocks[:, 0], up_blocks[:, 0], down_blocks[:, 0],
+      gate_cols[:, 0].T, gate_count.T, up_cols[:, 0].T, up_count.T, down_cols[:, 0].T, down_count.T)
 
 
 def fits(mesh, n_tok, gate_blocks, down_blocks):
@@ -342,7 +375,7 @@
     weights = (rows * (slots + 1) + down_blocks.shape[0] * (slots + 1) // 2) * gate_blocks.shape[3] ** 2 * 2
     return (mesh.shape["col"] == 2 and mesh.shape["rep"] == 2 and n_tok <= 128
             and slots == down_blocks.shape[2] and gate_blocks.shape[0] == down_blocks.shape[0]
-            and rows % 4 == 0 and down_blocks.shape[0] % (8 * CH) == 0 and weights <= 40 * 2**20)
+            and rows % 4 == 0 and down_blocks.shape[0] % (8 * CH) == 0 and weights <= 40 * 2**20 and rows <= 128)
 
 
 def solution(mesh):

time: 65.9 us -> 58.5 us (0.89)
  other arithmetic: 3.71 us -> 0 us
  local copies, waits for them, and re-layouts: 3.91 us -> 1.57 us
  Pallas kernels: 57.9 us -> 56.8 us
    eq x3 -> x0, local copies, waits for them, and re-layouts: 2.34 us -> none  [slot_table(): col_ids[:, 0, None, :] == jnp.arange(width, dtype=jnp.int32)[None, :, None]]
    lt x3 -> x0, other arithmetic: 2.18 us -> none  [slot_table(): live = slot[None, :] < live_count]
    pallas_call x1, Pallas kernels: 57.9 us -> 56.8 us  [fused(): pl.pallas_call(functools.partial(kernel, n_row), out_shape=jax.ShapeDtype...]
    reduce_sum x1 -> x0, other arithmetic: 0.88 us -> none  [slot_table(): return slots + jnp.sum(jnp.where(hit, slot - slots, 0), axis=2)]
where the time goes in v2:
time: 58.5 us; the launch traced here: 58.3 us
  Pallas kernels  56.8 us (97%)
  local copies, waits for them, and re-layouts  1.57 us (3%)
    pallas_call x1, Pallas kernels, fused(): pl.pallas_call(functools.partial(kernel, n_row), out_shape=jax.ShapeDtype...  56.8 us
    unnamed x1, local copies, waits for them, and re-layouts  1.57 us

profile of v2, /device:TPU:0, one launch (start us, length us, event | category | flops | bytes accessed | tf_op | source)
XLA Modules:
  0.0 58.3 jit_solution(3512926979554160015)
XLA Ops:
  0.0 56.8 %shard_map.100 = bf16[16,4096]{1,0:T(8,128)(2,1)} custom-call(bf16[16,4096]{1,0:T(8,128)(2,1)} %tok_ref.1, bf16[32,24,128,128]{3,2,1,0:T(8,128)(2,1)} %bitcast.15, bf16[32,24,128,128]{3,2,1,0:T(8,128)(2,1)} %bitcast.16, bf16[32,24,128,128]{3,2,1,0:T(8,128)(2,1)} %bitcast.17, s32[24,32]{1,0:T(8,128)} %bitcast.18, s32[1,32]{1,0:T(1,128)} %bitcast.21, ...), custom_call_target="tpu_custom_call" | custom-call | flops 6442450944 | bytes 37748736 | tf_op jit(solution)/shard_map/pallas_call | solution.py:328
  56.8 1.6 %copy.12 = bf16[16,4096]{1,0:T(8,128)(2,1)} copy(bf16[16,4096]{1,0:T(8,128)(2,1)} %shard_map.100) | data formatting | bytes 262144

commit v3 on v2

--- a/solution.py
+++ b/solution.py
@@ -85,28 +85,29 @@
     per = pairs // CH
     step = 2 * blk
 
+    peers = [(k, e) for k in range(n_row) for e in range(2) if (k, e) != (0, 0)]
+
+    def peer(k, e):
+        return {"row": lax.rem(r + k, n_row), "rep": lax.rem(p + e, 2)}
+
+    barrier = pltpu.get_barrier_semaphore()
+    for k, e in peers:
+        pl.semaphore_signal(barrier, inc=1, device_id=peer(k, e), device_id_type=MESH)
+    pl.semaphore_signal(barrier, inc=1, device_id={"col": nc}, device_id_type=MESH)
     loads = []
     for n, (w, src, nr) in enumerate(((wg, g_hbm, rows), (wu, u_hbm, rows), (wd, d_hbm, drows))):
         w[:, slots] = jnp.zeros((nr, blk, blk), BF)
-        for q in range(2):
-            hr = nr // 2
+        for q in range(4):
+            hr = nr // 4
             cp = pltpu.make_async_copy(
                 src.at[pl.ds(p * nr + q * hr, hr)],
                 w.at[pl.ds(q * hr, hr), pl.ds(0, slots)],
                 wsem.at[n, q],
             )
-            cp.start()
+            if n < 2:
+                cp.start()
             loads.append(cp)
 
-    peers = [(k, e) for k in range(n_row) for e in range(2) if (k, e) != (0, 0)]
-
-    def peer(k, e):
-        return {"row": lax.rem(r + k, n_row), "rep": lax.rem(p + e, 2)}
-
-    barrier = pltpu.get_barrier_semaphore()
-    for k, e in peers:
-        pl.semaphore_signal(barrier, inc=1, device_id=peer(k, e), device_id_type=MESH)
-    pl.semaphore_signal(barrier, inc=1, device_id={"col": nc}, device_id_type=MESH)
     pl.semaphore_wait(barrier, len(peers) + 1)
 
     me = p * n_row + r
@@ -132,8 +133,10 @@
     dfull[...] = jnp.zeros_like(dfull)
     mine.wait()
     table.wait()
-    for cp in loads[:4]:
+    for cp in loads[:8]:
         cp.wait()
+    for cp in loads[8:]:
+        cp.start()
     for cp in toks:
         cp.wait_recv()
 
@@ -172,15 +175,12 @@
 
     cw = step * per
 
-    def sib_part(h, quarter):
-        def body(u, _):
-            for v in range(per):
-                gate, up = both(np_ * hb + quarter * qb + 2 * (u * per + v))
-                ssend[h * CH + u, :, v * step:(v + 1) * step] = gate
-                ssend[h * CH + u, :, cw + v * step:cw + (v + 1) * step] = up
-            to_sibling(h * CH + u).start()
-            return 0
-        lax.fori_loop(0, CH, body, 0)
+    def sib_part(h, quarter, u):
+        for v in range(per):
+            gate, up = both(np_ * hb + quarter * qb + 2 * (u * per + v))
+            ssend[h * CH + u, :, v * step:(v + 1) * step] = gate
+            ssend[h * CH + u, :, cw + v * step:cw + (v + 1) * step] = up
+        to_sibling(h * CH + u).start()
 
     def own_part(u, quarter):
         for v in range(per):
@@ -188,9 +188,12 @@
             own[u, :, v * step:(v + 1) * step] = gate
             own[u, :, cw + v * step:cw + (v + 1) * step] = up
 
-    sib_part(0, nc)
+    sib_part(0, nc, 0)
 
     def col_body(u, _):
+        @pl.when(u + 1 < CH)
+        def _():
+            sib_part(0, nc, u + 1)
         own_part(u, nc)
         to_sibling(u).wait_recv()
         xsend[u] = (own[u] + srecv[u]).astype(BF)
@@ -198,9 +201,8 @@
         return 0
 
     lax.fori_loop(0, CH, col_body, 0)
-    sib_part(1, c)
-
     def keep_body(u, _):
+        sib_part(1, c, u)
         own_part(u, c)
         return 0
 
@@ -215,7 +217,7 @@
         hid_copy(u).start()
         return 0
 
-    for cp in loads[4:]:
+    for cp in loads[8:]:
         cp.wait()
     kc = dfull.shape[1]
 
@@ -351,7 +353,7 @@
             V((CH, half, oc), F32),
             V((CH, half, oc), BF),
             V((CH, n_row - 1, t, oc), BF),
-            dma((3, 2)),
+            dma((3, 4)),
             dma((2,)),
             dma((2 * n_row,)), dma((2 * n_row,)),
             dma((2 * CH,)), dma((2 * CH,)),
@@ -375,7 +377,7 @@
     weights = (rows * (slots + 1) + down_blocks.shape[0] * (slots + 1) // 2) * gate_blocks.shape[3] ** 2 * 2
     return (mesh.shape["col"] == 2 and mesh.shape["rep"] == 2 and n_tok <= 128
             and slots == down_blocks.shape[2] and gate_blocks.shape[0] == down_blocks.shape[0]
-            and rows % 4 == 0 and down_blocks.shape[0] % (8 * CH) == 0 and weights <= 40 * 2**20 and rows <= 128)
+            and rows % 8 == 0 and down_blocks.shape[0] % (8 * CH) == 0 and weights <= 40 * 2**20 and rows <= 128)
 
 
 def solution(mesh):

time: 58.5 us -> 57.7 us (0.986)
  Pallas kernels: 56.8 us -> 56 us
    pallas_call x1, Pallas kernels: 56.8 us -> 56 us  [fused(): pl.pallas_call(functools.partial(kernel, n_row), out_shape=jax.ShapeDtype...]
where the time goes in v3:
time: 57.7 us; the launch traced here: 57.6 us
  Pallas kernels  56 us (97%)
  local copies, waits for them, and re-layouts  1.57 us (3%)
    pallas_call x1, Pallas kernels, fused(): pl.pallas_call(functools.partial(kernel, n_row), out_shape=jax.ShapeDtype...  56 us
    unnamed x1, local copies, waits for them, and re-layouts  1.57 us

profile of v3, /device:TPU:0, one launch (start us, length us, event | category | flops | bytes accessed | tf_op | source)
XLA Modules:
  0.0 57.6 jit_solution(15186257159501497023)
XLA Ops:
  0.0 56.0 %shard_map.100 = bf16[16,4096]{1,0:T(8,128)(2,1)} custom-call(bf16[16,4096]{1,0:T(8,128)(2,1)} %tok_ref.1, bf16[32,24,128,128]{3,2,1,0:T(8,128)(2,1)} %bitcast.15, bf16[32,24,128,128]{3,2,1,0:T(8,128)(2,1)} %bitcast.16, bf16[32,24,128,128]{3,2,1,0:T(8,128)(2,1)} %bitcast.17, s32[24,32]{1,0:T(8,128)} %bitcast.18, s32[1,32]{1,0:T(1,128)} %bitcast.21, ...), custom_call_target="tpu_custom_call" | custom-call | flops 6442450944 | bytes 37748736 | tf_op jit(solution)/shard_map/pallas_call | solution.py:330
  56.0 1.6 %copy.12 = bf16[16,4096]{1,0:T(8,128)(2,1)} copy(bf16[16,4096]{1,0:T(8,128)(2,1)} %shard_map.100) | data formatting | bytes 262144
